TPU v7x, 32 devices: a whole 2x2x4 slice. The times are simulated.
32 devices in a mesh: row: 4 (over y, core), stn: 2 (over x), chan: 4 (over z).
Axes of the slice: x: 2, y: 2, z: 4, core: 2. Of those that a mesh axis runs over, the one named last changes fastest.
Arguments:
- visibility: float32 [2, 4096, 640], P(None, ('chan', 'row', 'stn')), parts along dimension 1, may hold values from -0.5 to 0.5
- uv_offset: float32 [2, 4096, 640], P(None, ('chan', 'row', 'stn')), parts along dimension 1, may hold values from -12 to 12
- aterm: bfloat16 [2, 2048, 1024], P(None, ('chan', 'stn')), parts along dimension 1, may hold values from -4 to 4
- station_pair: int32 [4096, 2], P(('chan', 'row', 'stn')), parts along dimension 0, may hold values from 0 to 511
- tile_of: int32 [4096], P(('chan', 'row', 'stn')), parts along dimension 0, may hold values from 0 to 16383, as said below
- vis_count: int32 [4096], P(('chan', 'row', 'stn')), parts along dimension 0, may hold values from 1 to 640
Outputs:
- sky: float32 [8, 4096, 4096], P('chan', ('row', 'stn')), parts along dimension 0
There are 4 independent parts, one for each index of `chan`. A program takes and returns all parts, laid end to end along the dimension named above; each array names one. Nothing has to cross between parts.
Inputs may be any that keep to these rules, and one draw needn't show every extreme that they name: `tile_of`: the owner of tile t is (t // 128 // 32) * 2 + (t % 128) // 64. Among the 128 subgrids of one device at most 32 have tiles of one owner, and in every draw some owner gets exactly 32 from every device.
All inputs are finite; a program needn't handle non-finite values.
Results may differ from a plain program's by a relative error of at most 0.0047.
Values may be sent and summed in bfloat16 or wider, within the bound.
A program may use at most 320 MiB of HBM per device.

v0:
```python
import math

import jax
import jax.numpy as jnp
from jax import lax
from jax.sharding import PartitionSpec as P

N = 4096
SUB = 32


HIGHEST = lax.Precision.HIGHEST


def centred_table(length):
    offsets = jnp.arange(length, dtype=jnp.int32) - length // 2
    turns = jnp.mod(offsets[:, None] * offsets[None, :], length).astype(jnp.float32) * (
        2.0 * math.pi / length
    )
    factor = 1.0 / math.sqrt(length)
    return (jnp.cos(turns) * factor, -jnp.sin(turns) * factor)


def complex_contraction(pattern, left_re, left_im, right_re, right_im):
    real_part = jnp.einsum(pattern, left_re, right_re, precision=HIGHEST) - jnp.einsum(
        pattern, left_im, right_im, precision=HIGHEST
    )
    imag_part = jnp.einsum(pattern, left_re, right_im, precision=HIGHEST) + jnp.einsum(
        pattern, left_im, right_re, precision=HIGHEST
    )
    return (real_part, imag_part)


def narrow_contraction(pattern, left_re, left_im, right_re, right_im):
    real_part = jnp.einsum(
        pattern, left_re, right_re, preferred_element_type=jnp.float32
    ) - jnp.einsum(pattern, left_im, right_im, preferred_element_type=jnp.float32)
    imag_part = jnp.einsum(
        pattern, left_re, right_im, preferred_element_type=jnp.float32
    ) + jnp.einsum(pattern, left_im, right_re, preferred_element_type=jnp.float32)
    return (real_part, imag_part)


def subgrid_block(
    values_re, values_im, coord_u, coord_v, counts, first_re, first_im, second_re, second_im
):
    side = SUB
    location_sequence = values_re.shape[1]
    pixels = (jnp.arange(side, dtype=jnp.float32) - side // 2) * (2.0 * math.pi / side)
    living = (jnp.arange(location_sequence, dtype=jnp.int32)[None, :] < counts[:, None]).astype(
        jnp.float32
    )
    values_re = values_re * living
    values_im = values_im * living
    angle_u = coord_u[:, None, :] * pixels[None, :, None]
    angle_v = coord_v[:, None, :] * pixels[None, :, None]
    cosine_u = jnp.cos(angle_u)
    sine_u = jnp.sin(angle_u)
    weighted_real = (values_re[:, None, :] * cosine_u - values_im[:, None, :] * sine_u).astype(
        jnp.bfloat16
    )
    weighted_imaginary = (values_re[:, None, :] * sine_u + values_im[:, None, :] * cosine_u).astype(
        jnp.bfloat16
    )
    image_real, image_imaginary = narrow_contraction(
        "hci,hzi->hcz",
        weighted_real,
        weighted_imaginary,
        jnp.cos(angle_v).astype(jnp.bfloat16),
        jnp.sin(angle_v).astype(jnp.bfloat16),
    )
    batch = image_real.shape[0]
    beam_re = (first_re * second_re + first_im * second_im).reshape(batch, side, side)
    beam_im = (first_im * second_re - first_re * second_im).reshape(batch, side, side)
    shaped_re = image_real * beam_re - image_imaginary * beam_im
    shaped_im = image_real * beam_im + image_imaginary * beam_re
    table_re, table_im = centred_table(side)
    half_re, half_im = complex_contraction("ap,bpq->baq", table_re, table_im, shaped_re, shaped_im)
    full_re, full_im = complex_contraction("baq,cq->bac", half_re, half_im, table_re, table_im)
    joined = jnp.concatenate(
        [full_re.reshape(batch, side * side), full_im.reshape(batch, side * side)], axis=1
    )
    return joined.astype(jnp.bfloat16)


def fourier_tables(length):
    first_len = 1 << (length.bit_length() - 1) // 2
    second_len = length // first_len
    first_idx = jnp.arange(first_len, dtype=jnp.int32)
    second_idx = jnp.arange(second_len, dtype=jnp.int32)
    first_turn = jnp.mod(first_idx[:, None] * first_idx[None, :], first_len).astype(jnp.float32) * (
        2.0 * math.pi / first_len
    )
    second_turn = jnp.mod(second_idx[:, None] * second_idx[None, :], second_len).astype(
        jnp.float32
    ) * (2.0 * math.pi / second_len)
    twist_turn = jnp.mod(first_idx[:, None] * second_idx[None, :], length).astype(jnp.float32) * (
        2.0 * math.pi / length
    )
    return (
        first_len,
        second_len,
        (jnp.cos(first_turn), jnp.sin(first_turn)),
        (jnp.cos(second_turn), jnp.sin(second_turn)),
        (jnp.cos(twist_turn), jnp.sin(twist_turn)),
    )


def fourier_last(real_part, imag_part):
    rows_here, length = real_part.shape
    first_len, second_len, first_tab, second_tab, twist_tab = fourier_tables(length)
    shaped_re = real_part.reshape(rows_here, first_len, second_len)
    shaped_im = imag_part.reshape(rows_here, first_len, second_len)
    middle_re, middle_im = complex_contraction(
        "rab,ak->rkb", shaped_re, shaped_im, first_tab[0], first_tab[1]
    )
    turned_re = middle_re * twist_tab[0] - middle_im * twist_tab[1]
    turned_im = middle_re * twist_tab[1] + middle_im * twist_tab[0]
    result_re, result_im = complex_contraction(
        "rkb,bj->rjk", turned_re, turned_im, second_tab[0], second_tab[1]
    )
    return (result_re.reshape(rows_here, length), result_im.reshape(rows_here, length))


def fourier_first_swapped(real_part, imag_part):
    length, columns = real_part.shape
    first_len, second_len, first_tab, second_tab, twist_tab = fourier_tables(length)
    shaped_re = real_part.reshape(first_len, second_len, columns)
    shaped_im = imag_part.reshape(first_len, second_len, columns)
    middle_re, middle_im = complex_contraction(
        "abm,ak->kbm", shaped_re, shaped_im, first_tab[0], first_tab[1]
    )
    twist_re = twist_tab[0][:, :, None]
    twist_im = twist_tab[1][:, :, None]
    turned_re = middle_re * twist_re - middle_im * twist_im
    turned_im = middle_re * twist_im + middle_im * twist_re
    result_re, result_im = complex_contraction(
        "kbm,bj->mjk", turned_re, turned_im, second_tab[0], second_tab[1]
    )
    return (result_re.reshape(columns, length), result_im.reshape(columns, length))


def shards(visibility, uv_offset, aterm, station_pair, tile_of, vis_count):
    sub_count = visibility.shape[1]
    row_devices = lax.axis_size("row")
    stn_devices = lax.axis_size("stn")
    owners = row_devices * stn_devices
    area = SUB * SUB
    every_station = lax.all_gather(aterm, "stn", axis=1, tiled=True)
    first = jnp.take(every_station, station_pair[:, 0], axis=1).astype(jnp.float32)
    second = jnp.take(every_station, station_pair[:, 1], axis=1).astype(jnp.float32)
    batch = math.gcd(sub_count, 32)

    def one_block(position):
        begin_at = position * batch
        values = lax.dynamic_slice_in_dim(visibility, begin_at, batch, 1)
        coords = lax.dynamic_slice_in_dim(uv_offset, begin_at, batch, 1)
        counts = lax.dynamic_slice_in_dim(vis_count, begin_at, batch, 0)
        first_here = lax.dynamic_slice_in_dim(first, begin_at, batch, 1)
        second_here = lax.dynamic_slice_in_dim(second, begin_at, batch, 1)
        return subgrid_block(
            values[0],
            values[1],
            coords[0],
            coords[1],
            counts,
            first_here[0],
            first_here[1],
            second_here[0],
            second_here[1],
        )

    uv_subgrids = lax.map(one_block, jnp.arange(sub_count // batch, dtype=jnp.int32)).reshape(
        sub_count, 2 * area
    )
    tiles_side = N // SUB
    tile_rows = tiles_side // row_devices
    tile_cols = tiles_side // stn_devices
    tile_row = tile_of // tiles_side
    tile_col = tile_of % tiles_side
    owner = tile_row // tile_rows * stn_devices + tile_col // tile_cols
    local_tile = tile_row % tile_rows * tile_cols + tile_col % tile_cols
    capacity = max(2, 2 * sub_count // owners)
    ordinal = jnp.arange(sub_count, dtype=jnp.int32)
    earlier = (owner[:, None] == owner[None, :]) & (ordinal[:, None] > ordinal[None, :])
    rank = jnp.sum(earlier.astype(jnp.int32), axis=1)
    slot = owner * capacity + rank
    outgoing = jnp.zeros((owners * capacity, 2 * area), jnp.bfloat16).at[slot].set(uv_subgrids)
    labels = jnp.full((owners * capacity,), -1, jnp.int32).at[slot].set(local_tile)
    arrived, arrived_tiles = (
        lax.all_to_all(
            outgoing.reshape(owners, capacity, 2 * area),
            ("row", "stn"),
            split_axis=0,
            concat_axis=0,
            tiled=True,
        ),
        lax.all_to_all(
            labels.reshape(owners, capacity),
            ("row", "stn"),
            split_axis=0,
            concat_axis=0,
            tiled=True,
        ),
    )
    arrived = arrived.reshape(owners * capacity, 2 * area)
    arrived_tiles = arrived_tiles.reshape(owners * capacity)
    tiles_here = tile_rows * tile_cols
    placing = (jnp.arange(tiles_here, dtype=jnp.int32)[:, None] == arrived_tiles[None, :]).astype(
        jnp.bfloat16
    )
    tile_sums = jnp.dot(placing, arrived, preferred_element_type=jnp.float32)
    slab = tile_sums.reshape(tile_rows, tile_cols, 2, SUB, SUB).transpose(2, 0, 3, 1, 4)
    slab = slab.reshape(2, tile_rows * SUB, tile_cols * SUB)
    rows_each = tile_rows * SUB // stn_devices
    whole_rows = lax.all_to_all(
        slab.reshape(2, stn_devices, rows_each, tile_cols * SUB),
        "stn",
        split_axis=1,
        concat_axis=3,
        tiled=True,
    )
    whole_rows = whole_rows.reshape(2, rows_each, N)
    along_re, along_im = fourier_last(whole_rows[0], whole_rows[1])
    stacked = jnp.stack([along_re, along_im])
    whole_cols = lax.all_to_all(stacked, ("row", "stn"), split_axis=2, concat_axis=1, tiled=True)
    result_re, result_im = fourier_first_swapped(whole_cols[0], whole_cols[1])
    return jnp.stack([result_re, result_im]) * (1.0 / N)


def solution(mesh):
    in_specs = (
        P(None, ("chan", "row", "stn"), None),
        P(None, ("chan", "row", "stn"), None),
        P(None, ("chan", "stn"), None),
        P(("chan", "row", "stn"), None),
        P(("chan", "row", "stn")),
        P(("chan", "row", "stn")),
    )
    out_specs = P("chan", ("row", "stn"), None)
    return jax.shard_map(shards, mesh=mesh, in_specs=in_specs, out_specs=out_specs, check_vma=False)
```

profile of v0, /device:TPU:0, one launch (start us, length us, event | category | flops | bytes accessed | tf_op | source)
XLA Modules:
  0.0 1373.6 jit_solution(5824984986908785561)
XLA Ops:
  18.3 27.5 %all-gather.2.cloned.1.call-done = bf16[2,512,1024]{2,0,1:T(2,128)(2,1)} async-done(((bf16[2,256,1024]{2,0,1:T(2,128)(2,1)}), bf16[2,512,1024]{2,0,1:T(2,128)(2,1)}) %all-gather.2.cloned.1.call-update) | async-done | bytes 2097168 | tf_op jit(solution)/shard_map/all_gather | solution.py:149
  54.1 373.7 %while.12 = (s32[]{:T(128)}, bf16[4,32,2048]{2,1,0:T(8,128)(2,1)}, s32[4]{0:T(128)}, s32[128]{0:T(128)}, f32[2,128,640]{2,1,0:T(8,128)}, /*index=5*/f32[2,128,64...) while((s32[]{:T(128)}, bf16[4,32,2048]{2,1,0:T(8,128)(2,1)}, ...), condition=%wide.region_3.5_spmd, body=%wide.region_2.4_spmd.sunk | while | flops 287891552 | bytes 8981371 | solution.py:173
  59.0 18.3 %fusion.339 = f32[32,32,32]{2,1,0:T(8,128)S(1)} fusion(f32[32,640]{1,0:T(8,128)S(1)} %get-tuple-element.261, f32[32]{0:T(128)S(1)} %add_multiply_fusion.2, f32[32,640]{1,0:T(8,128)S(1)} %get-tuple-element.262, f32[32,640]{1,0:T(8,128)S(1)} %get-tuple-element.263, f32[32,640]{1,0:T(8,128)S(1)} %get-tuple-element.264), kind=kOutput, calls=%fused_computation.19.clone.1 | convolution fusion | flops 46530560 | bytes 458880 | tf_op jit(solution)/shard_map/while/body/eval_jaxpr/hci,hzi->hcz/dot_general | solution.py:37
  77.3 19.6 %fusion.340 = f32[32,32,32]{2,1,0:T(8,128)} fusion(f32[32,32,32]{2,1,0:T(8,128)S(1)} %fusion.339, f32[32,640]{1,0:T(8,128)S(1)} %get-tuple-element.261, f32[32]{0:T(128)S(1)} %add_multiply_fusion.2, f32[32,640]{1,0:T(8,128)S(1)} %get-tuple-element.262, f32[32,640]{1,0:T(8,128)S(1)} %get-tuple-element.263, f32[32,640]{1,0:T(8,128)S(1)} %get-tuple-element.264), kind=kOutput, calls=%fused_computation.30.clone.1 | convolution fusion | flops 46563328 | bytes 589952 | tf_op jit(solution)/shard_map/while/body/eval_jaxpr/hci,hzi->hcz/dot_general | solution.py:35
  97.7 19.1 %fusion.341 = f32[32,32,32]{2,1,0:T(8,128)S(1)} fusion(f32[32,640]{1,0:T(8,128)} %copy-done.5, f32[32]{0:T(128)S(1)} %add_multiply_fusion.2, f32[32,640]{1,0:T(8,128)S(1)} %get-tuple-element.262, f32[32,640]{1,0:T(8,128)S(1)} %get-tuple-element.263, f32[32,640]{1,0:T(8,128)S(1)} %get-tuple-element.264), kind=kOutput, calls=%fused_computation.18.clone.1 | convolution fusion | flops 46530560 | bytes 458880 | tf_op jit(solution)/shard_map/while/body/eval_jaxpr/hci,hzi->hcz/dot_general | solution.py:38
  116.9 19.9 %multiply_add_fusion.8 = (f32[32,32,32]{2,1,0:T(8,128)S(1)}, f32[32,32,32]{2,1,0:T(8,128)S(1)}) fusion(f32[32,32,32]{2,1,0:T(8,128)S(1)} %add.467, f32[32,32,32]{2,1,0:T(8,128)} %fusion.340, f32[32,32,32]{2,1,0:T(8,128)S(1)} %sub.166, f32[32,32,32]{2,1,0:T(8,128)S(1)} %fusion.341, f32[32,640]{1,0:T(8,128)} %copy-done.5, ...), kind=kOutput, calls=%fused_computation.40.clone.1 | convolution fusion | flops 46759936 | bytes 1114240 | tf_op jit(solution)/shard_map/while/body/eval_jaxpr/hci,hzi->hcz/dot_general | solution.py:40
  151.0 18.5 %fusion.339 = f32[32,32,32]{2,1,0:T(8,128)S(1)} fusion(f32[32,640]{1,0:T(8,128)S(1)} %get-tuple-element.261, f32[32]{0:T(128)S(1)} %add_multiply_fusion.2, f32[32,640]{1,0:T(8,128)S(1)} %get-tuple-element.262, f32[32,640]{1,0:T(8,128)S(1)} %get-tuple-element.263, f32[32,640]{1,0:T(8,128)S(1)} %get-tuple-element.264), kind=kOutput, calls=%fused_computation.19.clone.1 | convolution fusion | flops 46530560 | bytes 458880 | tf_op jit(solution)/shard_map/while/body/eval_jaxpr/hci,hzi->hcz/dot_general | solution.py:37
  169.5 19.3 %fusion.340 = f32[32,32,32]{2,1,0:T(8,128)} fusion(f32[32,32,32]{2,1,0:T(8,128)S(1)} %fusion.339, f32[32,640]{1,0:T(8,128)S(1)} %get-tuple-element.261, f32[32]{0:T(128)S(1)} %add_multiply_fusion.2, f32[32,640]{1,0:T(8,128)S(1)} %get-tuple-element.262, f32[32,640]{1,0:T(8,128)S(1)} %get-tuple-element.263, f32[32,640]{1,0:T(8,128)S(1)} %get-tuple-element.264), kind=kOutput, calls=%fused_computation.30.clone.1 | convolution fusion | flops 46563328 | bytes 589952 | tf_op jit(solution)/shard_map/while/body/eval_jaxpr/hci,hzi->hcz/dot_general | solution.py:35
  189.7 19.3 %fusion.341 = f32[32,32,32]{2,1,0:T(8,128)S(1)} fusion(f32[32,640]{1,0:T(8,128)} %copy-done.5, f32[32]{0:T(128)S(1)} %add_multiply_fusion.2, f32[32,640]{1,0:T(8,128)S(1)} %get-tuple-element.262, f32[32,640]{1,0:T(8,128)S(1)} %get-tuple-element.263, f32[32,640]{1,0:T(8,128)S(1)} %get-tuple-element.264), kind=kOutput, calls=%fused_computation.18.clone.1 | convolution fusion | flops 46530560 | bytes 458880 | tf_op jit(solution)/shard_map/while/body/eval_jaxpr/hci,hzi->hcz/dot_general | solution.py:38
  209.0 19.7 %multiply_add_fusion.8 = (f32[32,32,32]{2,1,0:T(8,128)S(1)}, f32[32,32,32]{2,1,0:T(8,128)S(1)}) fusion(f32[32,32,32]{2,1,0:T(8,128)S(1)} %add.467, f32[32,32,32]{2,1,0:T(8,128)} %fusion.340, f32[32,32,32]{2,1,0:T(8,128)S(1)} %sub.166, f32[32,32,32]{2,1,0:T(8,128)S(1)} %fusion.341, f32[32,640]{1,0:T(8,128)} %copy-done.5, ...), kind=kOutput, calls=%fused_computation.40.clone.1 | convolution fusion | flops 46759936 | bytes 1114240 | tf_op jit(solution)/shard_map/while/body/eval_jaxpr/hci,hzi->hcz/dot_general | solution.py:40
  243.2 18.2 %fusion.339 = f32[32,32,32]{2,1,0:T(8,128)S(1)} fusion(f32[32,640]{1,0:T(8,128)S(1)} %get-tuple-element.261, f32[32]{0:T(128)S(1)} %add_multiply_fusion.2, f32[32,640]{1,0:T(8,128)S(1)} %get-tuple-element.262, f32[32,640]{1,0:T(8,128)S(1)} %get-tuple-element.263, f32[32,640]{1,0:T(8,128)S(1)} %get-tuple-element.264), kind=kOutput, calls=%fused_computation.19.clone.1 | convolution fusion | flops 46530560 | bytes 458880 | tf_op jit(solution)/shard_map/while/body/eval_jaxpr/hci,hzi->hcz/dot_general | solution.py:37
  261.4 19.5 %fusion.340 = f32[32,32,32]{2,1,0:T(8,128)} fusion(f32[32,32,32]{2,1,0:T(8,128)S(1)} %fusion.339, f32[32,640]{1,0:T(8,128)S(1)} %get-tuple-element.261, f32[32]{0:T(128)S(1)} %add_multiply_fusion.2, f32[32,640]{1,0:T(8,128)S(1)} %get-tuple-element.262, f32[32,640]{1,0:T(8,128)S(1)} %get-tuple-element.263, f32[32,640]{1,0:T(8,128)S(1)} %get-tuple-element.264), kind=kOutput, calls=%fused_computation.30.clone.1 | convolution fusion | flops 46563328 | bytes 589952 | tf_op jit(solution)/shard_map/while/body/eval_jaxpr/hci,hzi->hcz/dot_general | solution.py:35
  281.9 19.1 %fusion.341 = f32[32,32,32]{2,1,0:T(8,128)S(1)} fusion(f32[32,640]{1,0:T(8,128)} %copy-done.5, f32[32]{0:T(128)S(1)} %add_multiply_fusion.2, f32[32,640]{1,0:T(8,128)S(1)} %get-tuple-element.262, f32[32,640]{1,0:T(8,128)S(1)} %get-tuple-element.263, f32[32,640]{1,0:T(8,128)S(1)} %get-tuple-element.264), kind=kOutput, calls=%fused_computation.18.clone.1 | convolution fusion | flops 46530560 | bytes 458880 | tf_op jit(solution)/shard_map/while/body/eval_jaxpr/hci,hzi->hcz/dot_general | solution.py:38
  301.0 19.9 %multiply_add_fusion.8 = (f32[32,32,32]{2,1,0:T(8,128)S(1)}, f32[32,32,32]{2,1,0:T(8,128)S(1)}) fusion(f32[32,32,32]{2,1,0:T(8,128)S(1)} %add.467, f32[32,32,32]{2,1,0:T(8,128)} %fusion.340, f32[32,32,32]{2,1,0:T(8,128)S(1)} %sub.166, f32[32,32,32]{2,1,0:T(8,128)S(1)} %fusion.341, f32[32,640]{1,0:T(8,128)} %copy-done.5, ...), kind=kOutput, calls=%fused_computation.40.clone.1 | convolution fusion | flops 46759936 | bytes 1114240 | tf_op jit(solution)/shard_map/while/body/eval_jaxpr/hci,hzi->hcz/dot_general | solution.py:40
  335.1 18.3 %fusion.339 = f32[32,32,32]{2,1,0:T(8,128)S(1)} fusion(f32[32,640]{1,0:T(8,128)S(1)} %get-tuple-element.261, f32[32]{0:T(128)S(1)} %add_multiply_fusion.2, f32[32,640]{1,0:T(8,128)S(1)} %get-tuple-element.262, f32[32,640]{1,0:T(8,128)S(1)} %get-tuple-element.263, f32[32,640]{1,0:T(8,128)S(1)} %get-tuple-element.264), kind=kOutput, calls=%fused_computation.19.clone.1 | convolution fusion | flops 46530560 | bytes 458880 | tf_op jit(solution)/shard_map/while/body/eval_jaxpr/hci,hzi->hcz/dot_general | solution.py:37
  353.4 19.5 %fusion.340 = f32[32,32,32]{2,1,0:T(8,128)} fusion(f32[32,32,32]{2,1,0:T(8,128)S(1)} %fusion.339, f32[32,640]{1,0:T(8,128)S(1)} %get-tuple-element.261, f32[32]{0:T(128)S(1)} %add_multiply_fusion.2, f32[32,640]{1,0:T(8,128)S(1)} %get-tuple-element.262, f32[32,640]{1,0:T(8,128)S(1)} %get-tuple-element.263, f32[32,640]{1,0:T(8,128)S(1)} %get-tuple-element.264), kind=kOutput, calls=%fused_computation.30.clone.1 | convolution fusion | flops 46563328 | bytes 589952 | tf_op jit(solution)/shard_map/while/body/eval_jaxpr/hci,hzi->hcz/dot_general | solution.py:35
  373.8 19.1 %fusion.341 = f32[32,32,32]{2,1,0:T(8,128)S(1)} fusion(f32[32,640]{1,0:T(8,128)} %copy-done.5, f32[32]{0:T(128)S(1)} %add_multiply_fusion.2, f32[32,640]{1,0:T(8,128)S(1)} %get-tuple-element.262, f32[32,640]{1,0:T(8,128)S(1)} %get-tuple-element.263, f32[32,640]{1,0:T(8,128)S(1)} %get-tuple-element.264), kind=kOutput, calls=%fused_computation.18.clone.1 | convolution fusion | flops 46530560 | bytes 458880 | tf_op jit(solution)/shard_map/while/body/eval_jaxpr/hci,hzi->hcz/dot_general | solution.py:38
  392.9 19.9 %multiply_add_fusion.8 = (f32[32,32,32]{2,1,0:T(8,128)S(1)}, f32[32,32,32]{2,1,0:T(8,128)S(1)}) fusion(f32[32,32,32]{2,1,0:T(8,128)S(1)} %add.467, f32[32,32,32]{2,1,0:T(8,128)} %fusion.340, f32[32,32,32]{2,1,0:T(8,128)S(1)} %sub.166, f32[32,32,32]{2,1,0:T(8,128)S(1)} %fusion.341, f32[32,640]{1,0:T(8,128)} %copy-done.5, ...), kind=kOutput, calls=%fused_computation.40.clone.1 | convolution fusion | flops 46759936 | bytes 1114240 | tf_op jit(solution)/shard_map/while/body/eval_jaxpr/hci,hzi->hcz/dot_general | solution.py:40
  436.4 12.8 all-to-all-done.1
  449.7 13.3 convolution_bitcast_fusion
  463.0 44.8 %copy.149 = f32[2,32,32,64,32]{4,3,2,1,0:T(8,128)} copy(f32[2,32,32,64,32]{3,4,2,0,1:T(8,128)} %convolution_bitcast_fusion) | data formatting | bytes 33554432 | tf_op jit(solution)/shard_map/transpose | solution.py:213
  507.9 49.6 %reshape_reshape.3 = f32[2,2,512,2048]{3,2,1,0:T(8,128)} reshape(f32[2,32,32,64,32]{4,3,2,1,0:T(8,128)} %copy.149) | data formatting | bytes 33554432 | tf_op jit(solution)/shard_map/reshape;reshape | solution.py:217
  557.4 11.6 copy.150
  569.1 9.7 all-to-all-start.2
  579.0 182.2 %all-to-all-done.2 = f32[2,2,512,2048]{3,2,0,1:T(8,128)} async-done(((f32[2,2,512,2048]{3,2,0,1:T(8,128)}), f32[2,2,512,2048]{3,2,0,1:T(8,128)}, u32[]{:S(2)}, u32[]{:S(2)}) %all-to-all-start.2) | async-done | bytes 16777248 | tf_op jit(solution)/shard_map/all_to_all | solution.py:216
  761.1 16.8 %copy.151 = f32[2,2,512,2048]{2,3,1,0:T(8,128)} copy(f32[2,2,512,2048]{3,2,0,1:T(8,128)} %all-to-all-done.2) | data formatting | bytes 33554432 | tf_op jit(solution)/shard_map/all_to_all | solution.py:216
  784.8 13.3 fusion.129
  798.1 13.3 fusion.131
  811.4 13.1 fusion.133
  824.5 24.9 %subtract_bitcast_fusion.2 = (f32[512,64,64]{0,1,2:T(8,128)}, f32[512,64,64]{0,1,2:T(8,128)}) fusion(f32[64,64]{0,1:T(8,128)S(1)} %get-tuple-element.193, f32[64,64]{0,1:T(8,128)S(1)} %get-tuple-element.194, f32[64,512,64]{1,0,2:T(8,128)} %fusion.133, f32[64,512,64]{1,0,2:T(8,128)} %fusion.129, f32[64,512,64]{1,0,2:T(8,128)} %fusion.131, ...), kind=kOutput, calls=%fused_computation.134 | convolution fusion | flops 1627447296 | bytes 50364416 | tf_op jit(solution)/shard_map/rab,ak->rkb/dot_general | solution.py:25
  849.4 17.9 %fusion.123 = f32[64,512,64]{1,0,2:T(8,128)} fusion(f32[512,64,64]{0,1,2:T(8,128)} %get-tuple-element.184), kind=kOutput, calls=%fused_computation.153 | convolution fusion | flops 1610670080 | bytes 16777216 | tf_op jit(solution)/shard_map/rkb,bj->rjk/dot_general | solution.py:25
  867.4 12.5 fusion.121
  879.9 15.6 %subtract_bitcast_fusion.1 = f32[512,64,64]{0,1,2:T(8,128)} fusion(f32[64,512,64]{1,0,2:T(8,128)} %fusion.123, f32[512,64,64]{0,1,2:T(8,128)S(1)} %bitcast.180), kind=kOutput, calls=%fused_computation.132 | convolution fusion | flops 1612767232 | bytes 25165824 | tf_op jit(solution)/shard_map/rkb,bj->rjk/dot_general | solution.py:25
  895.5 11.5 copy.158
  906.9 13.9 %add_bitcast_fusion.1 = f32[512,64,64]{0,1,2:T(8,128)} fusion(f32[64,512,64]{1,0,2:T(8,128)S(1)} %fusion.121, f32[512,64,64]{0,1,2:T(8,128)S(1)} %bitcast.180), kind=kOutput, calls=%fused_computation.131 | convolution fusion | flops 1612767232 | bytes 25165824 | tf_op jit(solution)/shard_map/rkb,bj->rjk/dot_general | solution.py:28
  920.8 11.5 copy.161
  939.1 32.4 %copy.162 = f32[2,512,4096]{1,0,2:T(2,128)} copy(f32[2,512,4096]{1,2,0:T(8,128)S(1)} %pad_maximum_fusion) | data formatting | bytes 33554432 | tf_op jit(solution)/shard_map/stack | solution.py:225
  971.5 187.6 %all_to_all.44 = f32[2,512,4096]{1,0,2:T(2,128)S(1)} all-to-all(f32[2,512,4096]{1,0,2:T(2,128)} %copy.162), channel_id=1, replica_groups=mesh['row'=4,'stn'=2,'chan'=4] {'row','stn'}, dimensions={2} | all-to-all | bytes 33554432 | tf_op jit(solution)/shard_map/all_to_all | solution.py:226
  1179.8 17.7 %fusion.113 = f32[64,64,512]{2,0,1:T(8,128)} fusion(f32[64,64,512]{2,1,0:T(8,128)} %bitcast.181), kind=kOutput, calls=%fused_computation.143 | convolution fusion | flops 1610670080 | bytes 16777216 | tf_op jit(solution)/shard_map/abm,ak->kbm/dot_general | solution.py:28
  1197.4 13.3 fusion.115
  1219.9 17.9 %fusion.119 = f32[64,64,512]{2,0,1:T(8,128)} fusion(f32[64,64,512]{2,1,0:T(8,128)} %bitcast.183), kind=kOutput, calls=%fused_computation.149 | convolution fusion | flops 1610670080 | bytes 16777216 | tf_op jit(solution)/shard_map/abm,ak->kbm/dot_general | solution.py:25
  1237.8 25.0 %multiply_subtract_fusion.2 = (f32[64,64,512]{2,0,1:T(8,128)}, f32[64,64,512]{2,0,1:T(8,128)}) fusion(f32[64,64]{0,1:T(8,128)S(1)} %get-tuple-element.193, f32[64,64]{0,1:T(8,128)S(1)} %get-tuple-element.194, f32[64,64,512]{2,0,1:T(8,128)} %fusion.113, f32[64,64,512]{2,0,1:T(8,128)} %fusion.119, f32[64,64,512]{2,0,1:T(8,128)} %fusion.115, ...), kind=kOutput, calls=%fused_computation.130 | convolution fusion | flops 1627447296 | bytes 50364416 | tf_op jit(solution)/shard_map/abm,ak->kbm/dot_general | solution.py:28
  1262.8 18.1 %fusion.107 = f32[64,64,512]{2,0,1:T(8,128)} fusion(f32[64,64,512]{2,0,1:T(8,128)} %get-tuple-element.182), kind=kOutput, calls=%fused_computation.137 | convolution fusion | flops 1610670080 | bytes 16777216 | tf_op jit(solution)/shard_map/kbm,bj->mjk/dot_general | solution.py:25
  1281.0 12.5 fusion.105
  1293.5 15.8 %subtract_bitcast_fusion = f32[512,64,64]{0,1,2:T(8,128)} fusion(f32[64,64,512]{2,0,1:T(8,128)} %fusion.107, f32[64,64,512]{2,0,1:T(8,128)S(1)} %bitcast.178), kind=kOutput, calls=%fused_computation.128 | convolution fusion | flops 1612767232 | bytes 25165824 | tf_op jit(solution)/shard_map/kbm,bj->mjk/dot_general | solution.py:25
  1309.2 11.5 copy.172
  1320.8 13.6 add_bitcast_fusion
  1349.1 17.5 %copy.176 = f32[2,512,4096]{2,1,0:T(8,128)} copy(f32[2,512,4096]{1,2,0:T(8,128)} %maximum_multiply_fusion) | data formatting | bytes 33554432 | tf_op jit(solution)/shard_map/mul | solution.py:228
  (149 shorter events, 144.6 us)
Async XLA Ops:
  6.5 39.3 %all-gather.2.cloned.1.call-start = ((), (), s32[]{:S(2)}) async-start(), calls=%async_computation.4 | async-start | bytes 3145728 | tf_op jit(solution)/shard_map/all_gather | solution.py:149
  10.7 7.6 copy-start.6
  12.4 418.4 %all-to-all-start = ((s32[8,1,32]{2,1,0:T(1,128)}), s32[8,1,32]{2,1,0:T(1,128)}, u32[]{:S(2)}, u32[]{:S(2)}) async-start(s32[8,1,32]{2,1,0:T(1,128)} %all_to_all.31), calls=%async_computation | async-start | bytes 8192 | tf_op jit(solution)/shard_map/all_to_all | solution.py:198
  58.9 37.9 %copy-start.5 = (f32[32,640]{1,0:T(8,128)}, f32[32,640]{1,0:T(8,128)S(1)}, u32[]{:S(2)}) copy-start(f32[32,640]{1,0:T(8,128)S(1)} %get-tuple-element.261) | copy-start | bytes 245764 | tf_op jit(solution)/shard_map/while
  151.0 37.8 %copy-start.5 = (f32[32,640]{1,0:T(8,128)}, f32[32,640]{1,0:T(8,128)S(1)}, u32[]{:S(2)}) copy-start(f32[32,640]{1,0:T(8,128)S(1)} %get-tuple-element.261) | copy-start | bytes 245764 | tf_op jit(solution)/shard_map/while
  243.2 37.8 %copy-start.5 = (f32[32,640]{1,0:T(8,128)}, f32[32,640]{1,0:T(8,128)S(1)}, u32[]{:S(2)}) copy-start(f32[32,640]{1,0:T(8,128)S(1)} %get-tuple-element.261) | copy-start | bytes 245764 | tf_op jit(solution)/shard_map/while
  335.1 37.8 %copy-start.5 = (f32[32,640]{1,0:T(8,128)}, f32[32,640]{1,0:T(8,128)S(1)}, u32[]{:S(2)}) copy-start(f32[32,640]{1,0:T(8,128)S(1)} %get-tuple-element.261) | copy-start | bytes 245764 | tf_op jit(solution)/shard_map/while
  430.8 18.4 %all-to-all-start.1 = ((bf16[8,32,2048]{2,1,0:T(8,128)(2,1)}), bf16[8,32,2048]{2,1,0:T(8,128)(2,1)S(1)}, u32[]{:S(2)}, u32[]{:S(2)}) async-start(bf16[8,32,2048]{2,1,0:T(8,128)(2,1)} %bitcast.17), calls=%async_computation.1 | async-start | bytes 2097152 | tf_op jit(solution)/shard_map/all_to_all | solution.py:191
  569.1 192.1 %all-to-all-start.2 = ((f32[2,2,512,2048]{3,2,0,1:T(8,128)}), f32[2,2,512,2048]{3,2,0,1:T(8,128)}, u32[]{:S(2)}, u32[]{:S(2)}) async-start(f32[2,2,512,2048]{3,2,0,1:T(8,128)} %copy.150), calls=%async_computation.2 | async-start | bytes 33554432 | tf_op jit(solution)/shard_map/all_to_all | solution.py:216
  784.8 26.6 %copy-start.3 = (f32[1,1,512,2,2048]{2,4,3,1,0:T(8,128)}, f32[1,1,512,2,2048]{2,4,3,1,0:T(8,128)S(1)}, u32[]{:S(2)}) copy-start(f32[1,1,512,2,2048]{2,4,3,1,0:T(8,128)S(1)} %get-tuple-element.188) | copy-start | bytes 25165828
  849.4 17.9 %copy-start.2 = (f32[512,64,64]{0,1,2:T(8,128)S(1)}, f32[512,64,64]{0,1,2:T(8,128)}, u32[]{:S(2)}) copy-start(f32[512,64,64]{0,1,2:T(8,128)} %get-tuple-element.184) | copy-start | bytes 25165828
  849.4 30.4 %slice-start.2 = ((s8[8388608]{0:T(1024)(128)(4,1)}), s8[4194304]{0:T(1024)(128)(4,1)S(1)}, s32[]{:S(2)}) async-start(s8[8388608]{0:T(1024)(128)(4,1)} %bitcast.179), calls=%async_computation.7 | async-start | bytes 8388608
  867.4 12.5 slice-start.3
  1179.8 17.7 %copy-start = (f32[1,8,512,512]{3,2,1,0:T(8,128)S(1)}, f32[1,8,512,512]{3,2,1,0:T(8,128)}, u32[]{:S(2)}) copy-start(f32[1,8,512,512]{3,2,1,0:T(8,128)} %copy.166) | copy-start | bytes 25165828
  1262.8 18.1 %copy-start.1 = (f32[64,64,512]{2,0,1:T(8,128)S(1)}, f32[64,64,512]{2,0,1:T(8,128)}, u32[]{:S(2)}) copy-start(f32[64,64,512]{2,0,1:T(8,128)} %get-tuple-element.182) | copy-start | bytes 25165828
  1262.8 30.6 %slice-start = ((s8[8388608]{0:T(1024)(128)(4,1)}), s8[4194304]{0:T(1024)(128)(4,1)S(1)}, s32[]{:S(2)}) async-start(s8[8388608]{0:T(1024)(128)(4,1)} %bitcast.177), calls=%async_computation.5 | async-start | bytes 8388608
  1281.0 12.5 slice-start.1
  1334.4 8.4 copy-start.4
Sparse Core Ops, SparseCore 0:
  10.0 35.8 all-gather.1
where the time goes:
time: 1390 us; the launch traced here: 1370 us
  matrix products  611 us (44%)
  local copies, waits for them, and re-layouts  286 us (21%)
  waiting for transfers between devices  222 us (16%)
  blocking collectives  188 us (14%)
  other arithmetic  24.7 us (2%)
  starting transfers between devices  18.5 us (1%)
  between operations  13.9 us (1%)
    all_to_all x1, blocking collectives, shards(): lax.all_to_all(stacked, ('row', 'stn'), split_axis=2, concat_axis=1, tile...  188 us
    all_to_all x1, waiting for transfers between devices, shards(): lax.all_to_all(slab.reshape(2, stn_devices, rows_each, tile_cols * SUB),...  182 us
    dot_general x12, matrix products, complex_contraction(): jnp.einsum(pattern, left_re, right_re, precision=HIGHEST)  82.3 us
    dot_general x4, matrix products, narrow_contraction(): jnp.einsum(pattern, left_im, right_re, preferred_element_type=jnp.float32)  79.3 us
    dot_general x4, matrix products, narrow_contraction(): jnp.einsum(pattern, left_re, right_re, preferred_element_type=jnp.float32)  77.9 us
    dot_general x4, matrix products, narrow_contraction(): jnp.einsum(pattern, left_re, right_im, preferred_element_type=jnp.float32)  76.7 us
    dot_general x12, matrix products, complex_contraction(): jnp.einsum(pattern, left_re, right_im, precision=HIGHEST)  73.8 us
    dot_general x4, matrix products, narrow_contraction(): jnp.einsum(pattern, left_im, right_im, preferred_element_type=jnp.float32)  73.2 us
  transfers between devices with their start and end apart: 4, of which 3 were waited for; matrix products, arithmetic and copies ran while one was open for 28% of the time, Pallas kernels for 0%

commit v1 on v0

v1 whole, which is shorter than its diff:
```python
import math

import jax
import jax.numpy as jnp
import ml_dtypes
import numpy as np
from jax import lax
from jax.experimental import pallas as pl
from jax.experimental.pallas import tpu as pltpu
from jax.sharding import PartitionSpec as P

N = 4096
SUB = 32
TILES = N // SUB
BF16 = jnp.bfloat16
F32 = jnp.float32

SIN_POLY = tuple((-1) ** k * math.pi ** (2 * k + 1) / math.factorial(2 * k + 1) for k in range(6))
COS_POLY = tuple((-1) ** k * math.pi ** (2 * k) / math.factorial(2 * k) for k in range(7))


def unit_circle(turns):
    part = turns - jnp.round(turns)
    square = part * part
    sine = SIN_POLY[-1]
    for coefficient in SIN_POLY[-2::-1]:
        sine = sine * square + coefficient
    sine = sine * part
    cosine = COS_POLY[-1]
    for coefficient in COS_POLY[-2::-1]:
        cosine = cosine * square + coefficient
    return 1.0 - 2.0 * sine * sine, 2.0 * sine * cosine


def split_high_low(table):
    high = table.astype(ml_dtypes.bfloat16)
    low = (table - high.astype(np.float64)).astype(ml_dtypes.bfloat16)
    return high, low


def predict_kernel(vis_ref, off_ref, count_ref, out_ref):
    subs, slots = vis_ref.shape[1], vis_ref.shape[2]
    slot = lax.broadcasted_iota(jnp.int32, (subs, slots), 1)
    live = (slot < count_ref[...]).astype(F32)
    vis_re = vis_ref[0] * live
    vis_im = vis_ref[1] * live
    coord_u = off_ref[0]
    coord_v = off_ref[1]
    step_u = unit_circle(coord_u * (8.0 / SUB))
    step_v = unit_circle(coord_v * (8.0 / SUB))
    first = (lax.broadcasted_iota(jnp.int32, (8, slots), 0) - SUB // 2).astype(F32) * (1.0 / SUB)
    for i in range(subs):
        row = slice(i, i + 1)

        def wide(value):
            return jnp.broadcast_to(value[row, :], (8, slots))

        def climb(re, im, step):
            step_re, step_im = wide(step[0]), wide(step[1])
            res, ims = [re], [im]
            for _ in range(SUB // 8 - 1):
                re, im = re * step_re - im * step_im, re * step_im + im * step_re
                res.append(re)
                ims.append(im)
            return jnp.concatenate(res + ims, axis=0).astype(BF16)

        cos_u, sin_u = unit_circle(wide(coord_u) * first)
        value_re, value_im = wide(vis_re), wide(vis_im)
        left = climb(value_re * cos_u - value_im * sin_u, value_re * sin_u + value_im * cos_u, step_u)
        cos_v, sin_v = unit_circle(wide(coord_v) * first)
        right = climb(cos_v, sin_v, step_v)
        both = lax.dot_general(left, right, (((1,), (1,)), ((), ())), preferred_element_type=F32)
        out_ref[0, i] = both[:SUB, :SUB] - both[SUB:, SUB:]
        out_ref[1, i] = both[:SUB, SUB:] + both[SUB:, :SUB]


def predict(visibility, uv_offset, vis_count):
    subs, slots = visibility.shape[1:]
    block = 8
    return pl.pallas_call(
        predict_kernel,
        grid=(subs // block,),
        in_specs=[
            pl.BlockSpec((2, block, slots), lambda i: (0, i, 0)),
            pl.BlockSpec((2, block, slots), lambda i: (0, i, 0)),
            pl.BlockSpec((block, 1), lambda i: (i, 0)),
        ],
        out_specs=pl.BlockSpec((2, block, SUB, SUB), lambda i: (0, i, 0, 0)),
        out_shape=jax.ShapeDtypeStruct((2, subs, SUB, SUB), F32),
        compiler_params=pltpu.CompilerParams(vmem_limit_bytes=48 << 20),
        cost_estimate=pl.CostEstimate(
            flops=subs * slots * 64 * 64 * 8, bytes_accessed=subs * slots * 16, transcendentals=0
        ),
        name="predict",
    )(visibility, uv_offset, vis_count.reshape(subs, 1))


def small_transform_table():
    centred = np.arange(SUB) - SUB // 2
    turns = np.outer(centred, centred) % SUB
    axis = np.exp(-2j * np.pi * turns / SUB)
    full = np.einsum("ap,bq->abpq", axis, axis).reshape(SUB, SUB, SUB * SUB) / SUB
    re, im = full.real, full.imag
    table = np.stack(
        [np.concatenate([re, -im], axis=2), np.concatenate([im, re], axis=2)], axis=1
    )
    return table.reshape(2 * SUB * SUB, 2 * SUB * SUB)


def column_table(owners, width):
    turns = np.outer(np.arange(N), np.arange(SUB)) % N
    wave = np.exp(2j * np.pi * turns / N).reshape(owners, width, SUB)
    table = np.concatenate(
        [
            np.concatenate([wave.real, -wave.imag], axis=2),
            np.concatenate([wave.imag, wave.real], axis=2),
        ],
        axis=1,
    )
    return np.concatenate(split_high_low(table), axis=2)


def tile_row_table():
    turns = np.outer(np.arange(TILES), np.arange(TILES)) % TILES
    wave = np.exp(2j * np.pi * turns / TILES)
    table = np.concatenate(
        [
            np.concatenate([wave.real, wave.imag], axis=1),
            np.concatenate([-wave.imag, wave.real], axis=1),
        ],
        axis=0,
    )
    high, low = split_high_low(table)
    return np.concatenate([high, high, low], axis=0)


def twiddle_table():
    turns = np.outer(np.arange(SUB), np.arange(TILES)) % N
    wave = np.exp(2j * np.pi * turns / N) / N
    return np.stack([wave.real, wave.imag], axis=1).astype(np.float32)


def fourier(res, ims):
    count = len(res)
    if count == 1:
        return res, ims
    even_re, even_im = fourier(res[0::2], ims[0::2])
    odd_re, odd_im = fourier(res[1::2], ims[1::2])
    low_re, low_im, high_re, high_im = [], [], [], []
    for k in range(count // 2):
        a, b = odd_re[k], odd_im[k]
        if k == 0:
            t_re, t_im = a, b
        elif 4 * k == count:
            t_re, t_im = -b, a
        elif 8 * k == count:
            t_re, t_im = (a - b) * math.sqrt(0.5), (a + b) * math.sqrt(0.5)
        elif 8 * k == 3 * count:
            t_re, t_im = (a + b) * -math.sqrt(0.5), (a - b) * math.sqrt(0.5)
        else:
            c, s = math.cos(2 * math.pi * k / count), math.sin(2 * math.pi * k / count)
            t_re, t_im = a * c - b * s, a * s + b * c
        low_re.append(even_re[k] + t_re)
        low_im.append(even_im[k] + t_im)
        high_re.append(even_re[k] - t_re)
        high_im.append(even_im[k] - t_im)
    return low_re + high_re, low_im + high_im


def image_kernel(
    uv_ref, wave_ref, cos_ref, sin_ref, hot_ref, rows_ref, twiddle_ref, sky_ref, shifted, middle
):
    step = pl.program_id(0)
    senders, subs = uv_ref.shape[0], uv_ref.shape[2]
    width = middle.shape[2]
    period = cos_ref.shape[0]
    together = min(senders, max(1, 256 // subs))

    @pl.when(step < SUB)
    def _():
        for begin in range(0, senders, together):
            uv = jnp.concatenate([uv_ref[d] for d in range(begin, begin + together)], axis=1)
            waves = jnp.dot(
                wave_ref[...],
                jnp.concatenate([uv, uv], axis=0),
                preferred_element_type=F32,
            )
            lanes = slice(begin * subs, (begin + together) * subs)
            cosine, sine = cos_ref[:, lanes], sin_ref[:, lanes]
            for at in range(0, width, period):
                re = waves[at : at + period]
                im = waves[width + at : width + at + period]
                shifted[at : at + period, lanes] = (re * cosine - im * sine).astype(BF16)
                shifted[width + at : width + at + period, lanes] = (
                    re * sine + im * cosine
                ).astype(BF16)
        placed = jnp.dot(shifted[...], hot_ref[...], preferred_element_type=F32)
        placed = jnp.concatenate([placed[:width], placed[width:]], axis=1)
        high = placed.astype(BF16)
        low = (placed - high.astype(F32)).astype(BF16)
        along = jnp.dot(
            jnp.concatenate([high, low, high], axis=1), rows_ref[...], preferred_element_type=F32
        )
        turn_re, turn_im = twiddle_ref[0:1, :], twiddle_ref[1:2, :]
        re, im = along[:, :TILES], along[:, TILES:]
        middle[0, step] = re * turn_re - im * turn_im
        middle[1, step] = re * turn_im + im * turn_re

    @pl.when(step >= SUB)
    def _():
        rows = sky_ref.shape[1]
        base = (step - SUB) * rows

        @pl.loop(0, rows // 8)
        def _(i):
            here = pl.ds(pl.multiple_of(i * 8, 8), 8)
            there = pl.ds(pl.multiple_of(base + i * 8, 8), 8)
            res, ims = fourier(
                [middle[0, a, there, :] for a in range(SUB)],
                [middle[1, a, there, :] for a in range(SUB)],
            )
            for k in range(SUB):
                sky_ref[0, here, k * TILES : (k + 1) * TILES] = res[k]
                sky_ref[1, here, k * TILES : (k + 1) * TILES] = ims[k]


def to_sky(uv, wave, cosine, sine, hot, rows, twiddle):
    senders, _, planes, subs = uv.shape
    width = wave.shape[0] // 2
    every = senders * subs
    block = min(32, width)

    def whole(array):
        return pl.BlockSpec(array.shape, lambda i: (0,) * array.ndim)

    return pl.pallas_call(
        image_kernel,
        grid=(SUB + width // block,),
        in_specs=[
            pl.BlockSpec((senders, None, planes, subs), lambda i: (0, jnp.minimum(i, SUB - 1), 0, 0)),
            whole(wave),
            whole(cosine),
            whole(sine),
            whole(hot),
            whole(rows),
            pl.BlockSpec((None, 2, TILES), lambda i: (jnp.minimum(i, SUB - 1), 0, 0)),
        ],
        out_specs=pl.BlockSpec((2, block, N), lambda i: (0, jnp.maximum(i - SUB, 0), 0)),
        out_shape=jax.ShapeDtypeStruct((2, width, N), F32),
        scratch_shapes=[
            pltpu.VMEM((2 * width, every), BF16),
            pltpu.VMEM((2, SUB, width, TILES), F32),
        ],
        compiler_params=pltpu.CompilerParams(vmem_limit_bytes=56 << 20),
        name="to_sky",
    )(uv, wave, cosine, sine, hot, rows, twiddle)


def shards(visibility, uv_offset, aterm, station_pair, tile_of, vis_count):
    subs = visibility.shape[1]
    owners = lax.axis_size("row") * lax.axis_size("stn")
    area = SUB * SUB
    width = N // owners
    me = lax.axis_index("row") * lax.axis_size("stn") + lax.axis_index("stn")

    tiles = lax.all_gather(tile_of, ("row", "stn"), axis=0, tiled=True)
    every_station = lax.all_gather(aterm, "stn", axis=1, tiled=True)
    image = predict(visibility, uv_offset, vis_count).reshape(2, subs, area)

    first = jnp.take(every_station, station_pair[:, 0], axis=1).astype(F32)
    second = jnp.take(every_station, station_pair[:, 1], axis=1).astype(F32)
    beam_re = first[0] * second[0] + first[1] * second[1]
    beam_im = first[1] * second[0] - first[0] * second[1]
    shaped = jnp.concatenate(
        [image[0] * beam_re - image[1] * beam_im, image[0] * beam_im + image[1] * beam_re], axis=1
    )
    shaped_high = lax.reduce_precision(shaped, 8, 7)
    shaped_low = (shaped - shaped_high).astype(BF16)
    shaped_high = shaped_high.astype(BF16)
    table_high, table_low = (jnp.asarray(t) for t in split_high_low(small_transform_table()))

    def product(table, data):
        return lax.dot_general(table, data, (((1,), (1,)), ((), ())), preferred_element_type=F32)

    uv = (
        product(table_high, shaped_high)
        + product(table_high, shaped_low)
        + product(table_low, shaped_high)
    ).astype(BF16)
    gathered = lax.all_gather(uv.reshape(SUB, 2 * SUB, subs), ("row", "stn"), axis=0)

    period = min(TILES, width)
    columns = (me * width + jnp.arange(period, dtype=jnp.int32)) % TILES
    turns = ((columns[:, None] * (tiles % TILES)[None, :]) % TILES).astype(F32) * (
        2.0 * math.pi / TILES
    )
    hot = ((tiles // TILES)[:, None] == jnp.arange(TILES, dtype=jnp.int32)[None, :]).astype(BF16)
    wave = lax.dynamic_index_in_dim(
        jnp.asarray(column_table(owners, width)), me, axis=0, keepdims=False
    )
    return to_sky(
        gathered,
        wave,
        jnp.cos(turns),
        jnp.sin(turns),
        hot,
        jnp.asarray(tile_row_table()),
        jnp.asarray(twiddle_table()),
    )


def solution(mesh):
    in_specs = (
        P(None, ("chan", "row", "stn"), None),
        P(None, ("chan", "row", "stn"), None),
        P(None, ("chan", "stn"), None),
        P(("chan", "row", "stn"), None),
        P(("chan", "row", "stn")),
        P(("chan", "row", "stn")),
    )
    out_specs = P("chan", ("row", "stn"), None)
    return jax.shard_map(shards, mesh=mesh, in_specs=in_specs, out_specs=out_specs, check_vma=False)
```

time: 1390 us -> 191 us (0.14); the launches traced: 1370 us -> 190 us
  matrix products: 611 us -> 12.5 us
  local copies, waits for them, and re-layouts: 286 us -> 21.5 us
  waiting for transfers between devices: 222 us -> 31.8 us
  blocking collectives: 188 us -> 9.84 us
  Pallas kernels: 0 us -> 96.2 us
  other arithmetic: 24.7 us -> 4.96 us
  starting transfers between devices: 18.5 us -> 0.04 us
    dot_general x65 -> x3, matrix products: 611 us -> 12.5 us  [product(): lax.dot_general(table, data, (((1,), (1,)), ((), ())), preferred_element_...]
    all_to_all x3 -> x0, waiting for transfers between devices: 195 us -> none  [the longest x1 182 us: shards(): lax.all_to_all(slab.reshape(2, stn_devices, rows_each, tile_cols * SUB),...]
    all_to_all x1 -> x0, blocking collectives: 188 us -> none  [shards(): lax.all_to_all(stacked, ('row', 'stn'), split_axis=2, concat_axis=1, tile...]
    pallas_call x0 -> x2, Pallas kernels: none -> 96.2 us  [the longest x1 80 us: to_sky(): pl.pallas_call(image_kernel, grid=(SUB + width // block,), in_specs=[pl.B...]
    another operation x3 -> x0, local copies, waits for them, and re-layouts: 93.6 us -> none  [the longest x2 61.2 us: shards(): slab.reshape(2, stn_devices, rows_each, tile_cols * SUB)]
    transpose x1 -> x0, local copies, waits for them, and re-layouts: 44.8 us -> none  [shards(): tile_sums.reshape(tile_rows, tile_cols, 2, SUB, SUB)]
    slice x8 -> x3, local copies, waits for them, and re-layouts: 34.1 us -> 5.69 us  [the longest x2 4.42 us: shards(): image[1] * beam_im]
    sub x6 -> x0, local copies, waits for them, and re-layouts: 23.7 us -> none  [the longest x2 23 us: complex_contraction(): jnp.einsum(pattern, left_re, right_re, precision=HIGHEST)]
  transfers between devices with their start and end apart: 4 -> 2, of which waited for: 3 -> 2; matrix products, arithmetic and copies ran while one was open for 28% -> 7% of each run, Pallas kernels for 0% -> 9%
where the time goes in v1:
time: 191 us; the launch traced here: 190 us
  Pallas kernels  96.2 us (50%)
  waiting for transfers between devices  31.8 us (17%)
  local copies, waits for them, and re-layouts  21.5 us (11%)
  between operations  13.6 us (7%)
  matrix products  12.5 us (7%)
  blocking collectives  9.84 us (5%)
  other arithmetic  4.96 us (3%)
    pallas_call x1, Pallas kernels, to_sky(): pl.pallas_call(image_kernel, grid=(SUB + width // block,), in_specs=[pl.B...  80 us
    all_gather x1, waiting for transfers between devices, shards(): lax.all_gather(uv.reshape(SUB, 2 * SUB, subs), ('row', 'stn'), axis=0)  21.2 us
    pallas_call x1, Pallas kernels, predict(): pl.pallas_call(predict_kernel, grid=(subs // block,), in_specs=[pl.BlockS...  16.2 us
    dot_general x3, matrix products, product(): lax.dot_general(table, data, (((1,), (1,)), ((), ())), preferred_element_...  12.5 us
    all_gather x1, waiting for transfers between devices, shards(): every_station = lax.all_gather(aterm, 'stn', axis=1, tiled=True)  10.6 us
    all_gather x1, blocking collectives, shards(): tiles = lax.all_gather(tile_of, ('row', 'stn'), axis=0, tiled=True)  9.84 us
    unnamed x17, local copies, waits for them, and re-layouts  5.49 us
    slice x2, local copies, waits for them, and re-layouts, shards(): image[1] * beam_im  4.42 us
  transfers between devices with their start and end apart: 2, of which 2 were waited for; matrix products, arithmetic and copies ran while one was open for 7% of the time, Pallas kernels for 9%

profile of v1, /device:TPU:0, one launch (start us, length us, event | category | flops | bytes accessed | tf_op | source)
XLA Modules:
  0.0 190.4 jit_solution(7129624210282731777)
XLA Ops:
  6.5 0.0 all-gather.4.cloned.1.call-start
  6.5 3.3 %copy.58 = bf16[2,256,1024]{2,0,1:T(2,128)(2,1)} copy(bf16[2,256,1024]{2,1,0:T(8,128)(2,1)} %param.15) | data formatting | bytes 2097152 | tf_op args[2]
  9.8 0.0 all-gather.4.cloned.1.call-update
  9.8 0.0 all-gather.6.cloned.1.call-start
  9.9 0.8 copy.56.count_ref
  10.7 0.0 copy-start
  10.7 1.1 copy-done
  11.7 0.0 copy-start.1
  11.7 1.1 copy-done.1
  12.8 16.2 %predict.1 = f32[2,128,32,32]{3,2,1,0:T(8,128)S(1)} custom-call(f32[2,128,640]{2,1,0:T(8,128)S(1)} %copy-done, f32[2,128,640]{2,1,0:T(8,128)S(1)} %copy-done.1, s32[128,1]{1,0:T(8,128)S(1)} %copy.56.count_ref), custom_call_target="tpu_custom_call" | custom-call | flops 2684354560 | bytes 1310720 | tf_op jit(solution)/shard_map/predict/pallas_call | solution.py:80
  29.1 0.0 copy-start.2
  29.1 1.8 fusion.19
  30.8 2.7 %copy.62 = f32[1,128,32,32]{1,3,2,0:T(8,128)S(1)} copy(f32[1,128,32,32]{3,2,1,0:T(8,128)} %get-tuple-element.13) | data formatting | bytes 1048576 | tf_op jit(solution)/shard_map/slice | solution.py:275
  33.5 0.2 copy.63
  33.7 1.3 copy.57
  35.0 0.2 copy.61
  35.2 0.0 copy-done.2
  35.2 10.6 %all-gather.4.cloned.1.call-done = bf16[2,512,1024]{2,0,1:T(2,128)(2,1)} async-done(((bf16[2,256,1024]{2,0,1:T(2,128)(2,1)}), bf16[2,512,1024]{2,0,1:T(2,128)(2,1)}) %all-gather.4.cloned.1.call-update) | async-done | bytes 2097168 | tf_op jit(solution)/shard_map/all_gather | solution.py:267
  45.8 3.2 %gather_fusion.1 = bf16[128,2,1024]{2,1,0:T(2,128)(2,1)S(1)} fusion(bf16[2,512,1024]{2,0,1:T(2,128)(2,1)} %all-gather.4.cloned.1.call-done, s32[1024]{0:T(1024)S(1)} %pad_clamp_fusion), kind=kCustom, calls=%fused_computation.1.clone | custom fusion | bytes 1049088 | tf_op jit(solution)/shard_map/jit(_take)/gather | solution.py:271
  49.0 3.2 %gather_fusion = bf16[128,2,1024]{2,1,0:T(2,128)(2,1)S(1)} fusion(bf16[2,512,1024]{2,0,1:T(2,128)(2,1)} %all-gather.4.cloned.1.call-done, s32[1024]{0:T(1024)S(1)} %pad_clamp_fusion.1), kind=kCustom, calls=%fused_computation.clone | custom fusion | bytes 1049088 | tf_op jit(solution)/shard_map/jit(_take)/gather | solution.py:270
  52.3 0.3 bitcast_convert_fusion
  52.6 0.0 slice-start
  52.6 0.4 fusion.7
  52.9 0.2 fusion.8
  53.1 0.0 slice-start.1
  53.1 0.0 slice-start.2
  53.1 6.5 %fusion.12 = f32[128,2048]{1,0:T(8,128)S(1)} fusion(bf16[2048,2048]{1,0:T(8,128)(2,1)} %constant.85.clone, f32[128,1024]{1,0:T(8,128)S(1)} %fusion.8, f32[128,1024]{1,0:T(8,128)S(1)} %get-tuple-element.6), kind=kOutput, calls=%fused_computation.35 | convolution fusion | flops 1074528256 | bytes 10485760 | tf_op jit(solution)/shard_map/dot_general | solution.py:283
  59.6 0.0 slice-done
  59.7 0.0 slice-done.1
  59.7 0.0 slice-start.3
  59.7 2.9 %convolution_add_fusion.1 = f32[128,2048]{1,0:T(8,128)S(1)} fusion(f32[128,2048]{1,0:T(8,128)S(1)} %fusion.12, bf16[2048,2048]{1,0:T(8,128)(2,1)S(1)} %bitcast.38, f32[128,1024]{1,0:T(8,128)S(1)} %fusion.8, f32[128,1024]{1,0:T(8,128)S(1)} %get-tuple-element.6), kind=kOutput, calls=%fused_computation.3 | convolution fusion | flops 1075052544 | bytes 11534336 | tf_op jit(solution)/shard_map/dot_general | solution.py:283
  62.6 0.0 slice-done.2
  62.6 0.0 slice-done.3
  62.6 0.0 copy-start.3
  62.6 3.1 %fusion.1 = bf16[2048,128]{0,1:T(8,128)(2,1)S(1)} fusion(f32[128,2048]{1,0:T(8,128)S(1)} %convolution_add_fusion.1, bf16[2048,2048]{1,0:T(8,128)(2,1)S(1)} %bitcast.40, f32[128,1024]{1,0:T(8,128)S(1)} %fusion.8, f32[128,1024]{1,0:T(8,128)S(1)} %get-tuple-element.6), kind=kOutput, calls=%fused_computation.5 | convolution fusion | flops 1075052544 | bytes 11010048 | tf_op jit(solution)/shard_map/dot_general | solution.py:283
  65.7 1.0 copy.66
  66.7 0.0 all-gather.6.cloned.1.call-update
  66.7 0.0 copy-done.3
  66.8 9.8 %all-gather = s32[8,1,128]{2,1,0:T(1,128)S(1)} all-gather(s32[1,1,128]{2,1,0:T(1,128)S(1)} %bitcast.46), channel_id=1, replica_groups=mesh['row'=4,'stn'=2,'chan'=4] {'row','stn'}, dimensions={0}, use_global_device_ids=true | all-gather | bytes 4608 | tf_op jit(solution)/shard_map/all_gather | solution.py:266
  76.6 1.7 dynamic-slice_bitcast_fusion.wave_ref
  78.3 0.9 fusion.9.hot_ref
  79.2 3.2 %fusion.10 = (f32[128,1024]{1,0:T(8,128)}, f32[128,1024]{1,0:T(8,128)}) fusion(s32[1024]{0:T(1024)S(1)} %get-tuple-element.18, s32[128]{0:T(128)S(1)} %and_select_fusion), kind=kLoop, calls=%fused_computation.32 | loop fusion | flops 1835008 | bytes 1053184 | tf_op jit(solution)/shard_map/sin | solution.py:305
  82.4 21.2 %all-gather.6.cloned.1.call-done.uv_ref = bf16[8,32,64,128]{3,2,1,0:T(8,128)(2,1)} async-done(((bf16[1,32,64,128]{3,2,1,0:T(8,128)(2,1)}), bf16[8,32,64,128]{3,2,1,0:T(8,128)(2,1)}) %all-gather.6.cloned.1.call-update) | async-done | bytes 4194320 | tf_op jit(solution)/shard_map/all_gather | solution.py:290
  103.6 80.0 %to_sky.1 = f32[2,512,4096]{2,1,0:T(8,128)} custom-call(bf16[8,32,64,128]{3,2,1,0:T(8,128)(2,1)} %all-gather.6.cloned.1.call-done.uv_ref, bf16[1024,128]{1,0:T(8,128)(2,1)} %dynamic-slice_bitcast_fusion.wave_ref, f32[128,1024]{1,0:T(8,128)} %get-tuple-element.16.cos_ref, f32[128,1024]{1,0:T(8,128)} %get-tuple-element.15.sin_ref, ...), custom_call_target="tpu_custom_call" | custom-call | tf_op jit(solution)/shard_map/to_sky/pallas_call | solution.py:236
  (7 shorter events, 0.0 us)
Async XLA Ops:
  6.5 39.3 %all-gather.4.cloned.1.call-start = ((), (), s32[]{:S(2)}) async-start(), calls=%async_computation | async-start | bytes 3145728 | tf_op jit(solution)/shard_map/all_gather | solution.py:267
  9.8 93.8 %all-gather.6.cloned.1.call-start = ((), (), s32[]{:S(2)}) async-start(), calls=%async_computation.1 | async-start | bytes 4718592 | tf_op jit(solution)/shard_map/all_gather | solution.py:290
  10.7 1.1 copy-start
  11.7 1.1 copy-start.1
  29.1 6.1 %copy-start.2 = (s32[128,2]{0,1:T(2,128)S(1)}, s32[128,2]{0,1:T(2,128)}, u32[]{:S(2)}) copy-start(s32[128,2]{0,1:T(2,128)} %param.16) | copy-start | bytes 3076
  52.6 7.1 %slice-start = ((s8[8388608]{0:T(1024)(128)(4,1)}), s8[4194304]{0:T(1024)(128)(4,1)S(1)}, s32[]{:S(2)}) async-start(s8[8388608]{0:T(1024)(128)(4,1)} %bitcast.37), calls=%async_computation.2 | async-start | bytes 8388608
  53.1 6.6 %slice-start.1 = ((s8[8388608]{0:T(1024)(128)(4,1)}), s8[4194304]{0:T(1024)(128)(4,1)S(1)}, s32[]{:S(2)}) async-start(s8[8388608]{0:T(1024)(128)(4,1)} %bitcast.37), calls=%async_computation.3 | async-start | bytes 8388608
  53.1 9.5 %slice-start.2 = ((s8[8388608]{0:T(1024)(128)(4,1)}), s8[4194304]{0:T(1024)(128)(4,1)S(1)}, s32[]{:S(2)}) async-start(s8[8388608]{0:T(1024)(128)(4,1)} %bitcast.39), calls=%async_computation.4 | async-start | bytes 8388608
  59.7 2.9 %slice-start.3 = ((s8[8388608]{0:T(1024)(128)(4,1)}), s8[4194304]{0:T(1024)(128)(4,1)S(1)}, s32[]{:S(2)}) async-start(s8[8388608]{0:T(1024)(128)(4,1)} %bitcast.39), calls=%async_computation.5 | async-start | bytes 8388608
  62.6 4.1 %copy-start.3 = (s32[128]{0:T(128)S(1)}, s32[128]{0:T(128)}, u32[]{:S(2)}) copy-start(s32[128]{0:T(128)} %param.17) | copy-start | bytes 1540
Sparse Core Ops, SparseCore 0:
  10.0 35.8 all-gather.3
  66.9 36.7 all-gather.5

commit v2 on v1

--- a/solution.py
+++ b/solution.py
@@ -118,20 +118,6 @@
         axis=1,
     )
     return np.concatenate(split_high_low(table), axis=2)
-
-
-def tile_row_table():
-    turns = np.outer(np.arange(TILES), np.arange(TILES)) % TILES
-    wave = np.exp(2j * np.pi * turns / TILES)
-    table = np.concatenate(
-        [
-            np.concatenate([wave.real, wave.imag], axis=1),
-            np.concatenate([-wave.imag, wave.real], axis=1),
-        ],
-        axis=0,
-    )
-    high, low = split_high_low(table)
-    return np.concatenate([high, high, low], axis=0)
 
 
 def twiddle_table():
@@ -167,93 +153,141 @@
     return low_re + high_re, low_im + high_im
 
 
-def image_kernel(
-    uv_ref, wave_ref, cos_ref, sin_ref, hot_ref, rows_ref, twiddle_ref, sky_ref, shifted, middle
-):
-    step = pl.program_id(0)
+def columns_of_one_row(uv_ref, wave_ref, cos_ref, sin_ref, rows_ref, twiddle_ref, shifted):
     senders, subs = uv_ref.shape[0], uv_ref.shape[2]
-    width = middle.shape[2]
+    width, every = shifted.shape[0], shifted.shape[1] // 2
     period = cos_ref.shape[0]
     together = min(senders, max(1, 256 // subs))
-
-    @pl.when(step < SUB)
+    for begin in range(0, senders, together):
+        uv = jnp.concatenate([uv_ref[d] for d in range(begin, begin + together)], axis=1)
+        waves = jnp.dot(
+            wave_ref[...], jnp.concatenate([uv, uv], axis=0), preferred_element_type=F32
+        )
+        first, last = begin * subs, (begin + together) * subs
+        cosine, sine = cos_ref[:, first:last], sin_ref[:, first:last]
+        for at in range(0, width, period):
+            re = waves[at : at + period]
+            im = waves[width + at : width + at + period]
+            shifted[at : at + period, first:last] = (re * cosine - im * sine).astype(BF16)
+            shifted[at : at + period, every + first : every + last] = (
+                re * sine + im * cosine
+            ).astype(BF16)
+    along = jnp.dot(shifted[...], rows_ref[...], preferred_element_type=F32)
+    turn_re, turn_im = twiddle_ref[0:1, :], twiddle_ref[1:2, :]
+    re, im = along[:, :TILES], along[:, TILES:]
+    return re * turn_re - im * turn_im, re * turn_im + im * turn_re
+
+
+def early_kernel(*refs):
+    *inputs, middle_ref, shifted = refs
+    middle_ref[0], middle_ref[1] = columns_of_one_row(*inputs, shifted)
+
+
+def late_kernel(*refs):
+    *inputs, early_ref, sky_ref, shifted, middle = refs
+    step = pl.program_id(0)
+    steps = middle.shape[1]
+
+    @pl.when(step < steps)
     def _():
-        for begin in range(0, senders, together):
-            uv = jnp.concatenate([uv_ref[d] for d in range(begin, begin + together)], axis=1)
-            waves = jnp.dot(
-                wave_ref[...],
-                jnp.concatenate([uv, uv], axis=0),
-                preferred_element_type=F32,
-            )
-            lanes = slice(begin * subs, (begin + together) * subs)
-            cosine, sine = cos_ref[:, lanes], sin_ref[:, lanes]
-            for at in range(0, width, period):
-                re = waves[at : at + period]
-                im = waves[width + at : width + at + period]
-                shifted[at : at + period, lanes] = (re * cosine - im * sine).astype(BF16)
-                shifted[width + at : width + at + period, lanes] = (
-                    re * sine + im * cosine
-                ).astype(BF16)
-        placed = jnp.dot(shifted[...], hot_ref[...], preferred_element_type=F32)
-        placed = jnp.concatenate([placed[:width], placed[width:]], axis=1)
-        high = placed.astype(BF16)
-        low = (placed - high.astype(F32)).astype(BF16)
-        along = jnp.dot(
-            jnp.concatenate([high, low, high], axis=1), rows_ref[...], preferred_element_type=F32
-        )
-        turn_re, turn_im = twiddle_ref[0:1, :], twiddle_ref[1:2, :]
-        re, im = along[:, :TILES], along[:, TILES:]
-        middle[0, step] = re * turn_re - im * turn_im
-        middle[1, step] = re * turn_im + im * turn_re
-
-    @pl.when(step >= SUB)
+        middle[0, step], middle[1, step] = columns_of_one_row(*inputs, shifted)
+
+    @pl.when(step >= steps)
     def _():
         rows = sky_ref.shape[1]
-        base = (step - SUB) * rows
+        base = (step - steps) * rows
 
         @pl.loop(0, rows // 8)
         def _(i):
             here = pl.ds(pl.multiple_of(i * 8, 8), 8)
             there = pl.ds(pl.multiple_of(base + i * 8, 8), 8)
             res, ims = fourier(
-                [middle[0, a, there, :] for a in range(SUB)],
-                [middle[1, a, there, :] for a in range(SUB)],
+                *(
+                    [early_ref[c, a, here, :] for a in range(SUB - steps)]
+                    + [middle[c, a, there, :] for a in range(steps)]
+                    for c in range(2)
+                )
             )
             for k in range(SUB):
                 sky_ref[0, here, k * TILES : (k + 1) * TILES] = res[k]
                 sky_ref[1, here, k * TILES : (k + 1) * TILES] = ims[k]
 
 
-def to_sky(uv, wave, cosine, sine, hot, rows, twiddle):
+def step_specs(uv, wave, cosine, sine, rows, twiddle, begin, steps):
     senders, _, planes, subs = uv.shape
-    width = wave.shape[0] // 2
+
+    def whole(array):
+        return pl.BlockSpec(array.shape, lambda i: (0,) * array.ndim)
+
+    return [
+        pl.BlockSpec((senders, None, planes, subs), lambda i: (0, jnp.minimum(i, steps - 1), 0, 0)),
+        whole(wave),
+        whole(cosine),
+        whole(sine),
+        whole(rows),
+        pl.BlockSpec((None, 2, TILES), lambda i: (begin + jnp.minimum(i, steps - 1), 0, 0)),
+    ]
+
+
+def early_rows(uv, *tables):
+    senders, steps, _, subs = uv.shape
+    width = tables[0].shape[0] // 2
+    every = senders * subs
+    return pl.pallas_call(
+        early_kernel,
+        grid=(steps,),
+        in_specs=step_specs(uv, *tables, 0, steps),
+        out_specs=pl.BlockSpec((2, None, width, TILES), lambda i: (0, i, 0, 0)),
+        out_shape=jax.ShapeDtypeStruct((2, steps, width, TILES), F32),
+        scratch_shapes=[pltpu.VMEM((width, 2 * every), BF16)],
+        compiler_params=pltpu.CompilerParams(vmem_limit_bytes=56 << 20),
+        cost_estimate=pl.CostEstimate(
+            flops=steps * 4 * every * width * 1024, bytes_accessed=16 << 20, transcendentals=0
+        ),
+        name="early_rows",
+    )(uv, *tables)
+
+
+def late_rows_to_sky(uv, *tables_and_early):
+    *tables, early = tables_and_early
+    senders, steps, _, subs = uv.shape
+    width = tables[0].shape[0] // 2
     every = senders * subs
     block = min(32, width)
-
-    def whole(array):
-        return pl.BlockSpec(array.shape, lambda i: (0,) * array.ndim)
-
     return pl.pallas_call(
-        image_kernel,
-        grid=(SUB + width // block,),
-        in_specs=[
-            pl.BlockSpec((senders, None, planes, subs), lambda i: (0, jnp.minimum(i, SUB - 1), 0, 0)),
-            whole(wave),
-            whole(cosine),
-            whole(sine),
-            whole(hot),
-            whole(rows),
-            pl.BlockSpec((None, 2, TILES), lambda i: (jnp.minimum(i, SUB - 1), 0, 0)),
-        ],
-        out_specs=pl.BlockSpec((2, block, N), lambda i: (0, jnp.maximum(i - SUB, 0), 0)),
+        late_kernel,
+        grid=(steps + width // block,),
+        in_specs=step_specs(uv, *tables, SUB - steps, steps)
+        + [
+            pl.BlockSpec(
+                (2, SUB - steps, block, TILES), lambda i: (0, 0, jnp.maximum(i - steps, 0), 0)
+            )
+        ],
+        out_specs=pl.BlockSpec((2, block, N), lambda i: (0, jnp.maximum(i - steps, 0), 0)),
         out_shape=jax.ShapeDtypeStruct((2, width, N), F32),
         scratch_shapes=[
-            pltpu.VMEM((2 * width, every), BF16),
-            pltpu.VMEM((2, SUB, width, TILES), F32),
+            pltpu.VMEM((width, 2 * every), BF16),
+            pltpu.VMEM((2, steps, width, TILES), F32),
         ],
         compiler_params=pltpu.CompilerParams(vmem_limit_bytes=56 << 20),
-        name="to_sky",
-    )(uv, wave, cosine, sine, hot, rows, twiddle)
+        name="late_rows_to_sky",
+    )(uv, *tables, early)
+
+
+def stations_and_places(aterm, pairs):
+    here = aterm.shape[1]
+    rows, sides = lax.axis_size("row"), lax.axis_size("stn")
+    if sides != 2 or rows % 2 or here % 2:
+        return lax.all_gather(aterm, "stn", axis=1, tiled=True), pairs
+    half = here // 2
+    parity = lax.axis_index("row") % 2
+    mine = lax.dynamic_slice_in_dim(aterm, parity * half, half, 1)
+    fetched = lax.ppermute(mine, "stn", [(0, 1), (1, 0)])
+    passed = lax.ppermute(fetched, "row", [(i, i ^ 1) for i in range(rows)])
+    own = pairs // here == lax.axis_index("stn")
+    inside = pairs % here
+    far = here + jnp.where(inside // half == parity, 0, half) + inside % half
+    return jnp.concatenate([aterm, fetched, passed], axis=1), jnp.where(own, inside, far)
 
 
 def shards(visibility, uv_offset, aterm, station_pair, tile_of, vis_count):
@@ -264,11 +298,11 @@
     me = lax.axis_index("row") * lax.axis_size("stn") + lax.axis_index("stn")
 
     tiles = lax.all_gather(tile_of, ("row", "stn"), axis=0, tiled=True)
-    every_station = lax.all_gather(aterm, "stn", axis=1, tiled=True)
+    every_station, places = stations_and_places(aterm, station_pair)
     image = predict(visibility, uv_offset, vis_count).reshape(2, subs, area)
 
-    first = jnp.take(every_station, station_pair[:, 0], axis=1).astype(F32)
-    second = jnp.take(every_station, station_pair[:, 1], axis=1).astype(F32)
+    first = jnp.take(every_station, places[:, 0], axis=1).astype(F32)
+    second = jnp.take(every_station, places[:, 1], axis=1).astype(F32)
     beam_re = first[0] * second[0] + first[1] * second[1]
     beam_im = first[1] * second[0] - first[0] * second[1]
     shaped = jnp.concatenate(
@@ -287,26 +321,35 @@
         + product(table_high, shaped_low)
         + product(table_low, shaped_high)
     ).astype(BF16)
-    gathered = lax.all_gather(uv.reshape(SUB, 2 * SUB, subs), ("row", "stn"), axis=0)
+    uv = uv.reshape(SUB, 2 * SUB, subs)
+    cut = 3 * SUB // 8
+    uv_early = lax.all_gather(uv[:cut], ("row", "stn"), axis=0)
 
     period = min(TILES, width)
     columns = (me * width + jnp.arange(period, dtype=jnp.int32)) % TILES
     turns = ((columns[:, None] * (tiles % TILES)[None, :]) % TILES).astype(F32) * (
         2.0 * math.pi / TILES
     )
-    hot = ((tiles // TILES)[:, None] == jnp.arange(TILES, dtype=jnp.int32)[None, :]).astype(BF16)
+    lines = jnp.arange(TILES, dtype=jnp.int32)
+    row_turns = (((tiles // TILES)[:, None] * lines[None, :]) % TILES).astype(F32) * (
+        2.0 * math.pi / TILES
+    )
+    row_cos, row_sin = jnp.cos(row_turns), jnp.sin(row_turns)
+    rows = jnp.concatenate(
+        [
+            jnp.concatenate([row_cos, row_sin], axis=1),
+            jnp.concatenate([-row_sin, row_cos], axis=1),
+        ],
+        axis=0,
+    ).astype(BF16)
     wave = lax.dynamic_index_in_dim(
         jnp.asarray(column_table(owners, width)), me, axis=0, keepdims=False
     )
-    return to_sky(
-        gathered,
-        wave,
-        jnp.cos(turns),
-        jnp.sin(turns),
-        hot,
-        jnp.asarray(tile_row_table()),
-        jnp.asarray(twiddle_table()),
-    )
+    tables = (wave, jnp.cos(turns), jnp.sin(turns), rows, jnp.asarray(twiddle_table()))
+    uv_rest, tables = lax.optimization_barrier((uv[cut:], tables))
+    uv_late = lax.all_gather(uv_rest, ("row", "stn"), axis=0)
+    early = early_rows(uv_early, *tables)
+    return late_rows_to_sky(uv_late, *tables, early)
 
 
 def solution(mesh):

time: 191 us -> 184 us (0.963)
  waiting for transfers between devices: 31.8 us -> 12.7 us
  local copies, waits for them, and re-layouts: 21.5 us -> 24.6 us
  starting transfers between devices: 0.04 us -> 3.05 us
  other arithmetic: 4.96 us -> 7.67 us
  Pallas kernels: 96.2 us -> 98.5 us
    all_gather x2, waiting for transfers between devices: 31.8 us -> 12.7 us  [the longest x1 6.33 us: shards(): uv_early = lax.all_gather(uv[:cut], ('row', 'stn'), axis=0)]
    ppermute x0 -> x2, starting transfers between devices: none -> 3.01 us  [the longest x1 2.94 us: stations_and_places(): fetched = lax.ppermute(mine, 'stn', [(0, 1), (1, 0)])]
    another operation x0 -> x1, other arithmetic: none -> 2.51 us
    pallas_call x1 -> x2, Pallas kernels: 80 us -> 82.2 us  [the longest x1 56.4 us: late_rows_to_sky(): pl.pallas_call(late_kernel, grid=(steps + width // block,), in_specs=step...]
    unnamed x17 -> x20, local copies, waits for them, and re-layouts: 5.49 us -> 6.2 us
  transfers between devices with their start and end apart: 2 -> 4, of which waited for: 2 -> 2; matrix products, arithmetic and copies ran while one was open for 7% -> 10% of each run, Pallas kernels for 9% -> 23%
where the time goes in v2:
time: 184 us; the launch traced here: 183 us
  Pallas kernels  98.5 us (54%)
  local copies, waits for them, and re-layouts  24.6 us (13%)
  between operations  13.7 us (7%)
  waiting for transfers between devices  12.7 us (7%)
  matrix products  12.5 us (7%)
  blocking collectives  10.5 us (6%)
  other arithmetic  7.67 us (4%)
  starting transfers between devices  3.05 us (2%)
    pallas_call x1, Pallas kernels, late_rows_to_sky(): pl.pallas_call(late_kernel, grid=(steps + width // block,), in_specs=step...  56.4 us
    pallas_call x1, Pallas kernels, early_rows(): pl.pallas_call(early_kernel, grid=(steps,), in_specs=step_specs(uv, *tabl...  25.8 us
    pallas_call x1, Pallas kernels, predict(): pl.pallas_call(predict_kernel, grid=(subs // block,), in_specs=[pl.BlockS...  16.3 us
    dot_general x3, matrix products, product(): lax.dot_general(table, data, (((1,), (1,)), ((), ())), preferred_element_...  12.5 us
    all_gather x1, blocking collectives, shards(): tiles = lax.all_gather(tile_of, ('row', 'stn'), axis=0, tiled=True)  10.5 us
    all_gather x1, waiting for transfers between devices, shards(): uv_early = lax.all_gather(uv[:cut], ('row', 'stn'), axis=0)  6.33 us
    all_gather x1, waiting for transfers between devices, shards(): uv_late = lax.all_gather(uv_rest, ('row', 'stn'), axis=0)  6.32 us
    unnamed x20, local copies, waits for them, and re-layouts  6.2 us
  transfers between devices with their start and end apart: 4, of which 2 were waited for; matrix products, arithmetic and copies ran while one was open for 10% of the time, Pallas kernels for 23%

profile of v2, /device:TPU:0, one launch (start us, length us, event | category | flops | bytes accessed | tf_op | source)
XLA Modules:
  0.0 183.2 jit_solution(4127154779154204604)
XLA Ops:
  6.5 4.0 %fusion.29 = (bf16[2,256,1024]{2,0,1:T(2,128)(2,1)S(1)}, bf16[2,512,1024]{2,0,1:T(2,128)(2,1)}) fusion(bf16[2,256,1024]{2,1,0:T(8,128)(2,1)} %param.14), kind=kLoop, calls=%fused_computation.88 | loop fusion | bytes 3145728 | tf_op args[2]
  10.5 1.2 constant_dynamic-slice_fusion
  11.7 2.9 %collective-permute-start = (bf16[2,128,1024]{2,0,1:T(2,128)(2,1)}, bf16[2,128,1024]{2,0,1:T(2,128)(2,1)}, u32[]{:S(2)}, u32[]{:S(2)}) collective-permute-start(bf16[2,128,1024]{2,0,1:T(2,128)(2,1)} %constant_dynamic-slice_fusion), channel_id=1, source_target_pairs={{0,4},{4,0},{1,5},{5,1},{2,6},{6,2},{3,7},{7,3},{8,12},{12,8},{9,1... | collective-permute-start | bytes 1572872 | tf_op jit(solution)/shard_map/ppermute | solution.py:285
  14.6 0.0 copy-done.3
  14.6 0.1 copy.62.count_ref
  14.7 0.0 copy-done
  14.7 16.3 %predict.1 = f32[2,128,32,32]{3,2,1,0:T(8,128)S(1)} custom-call(f32[2,128,640]{2,1,0:T(8,128)S(1)} %copy-done, f32[2,128,640]{2,1,0:T(8,128)S(1)} %copy-done.1, s32[128,1]{1,0:T(8,128)S(1)} %copy.62.count_ref), custom_call_target="tpu_custom_call" | custom-call | flops 2684354560 | bytes 1310720 | tf_op jit(solution)/shard_map/predict/pallas_call | solution.py:80
  31.0 1.8 fusion.28
  32.8 2.7 %copy.69 = f32[1,128,32,32]{1,3,2,0:T(8,128)S(1)} copy(f32[1,128,32,32]{3,2,1,0:T(8,128)} %get-tuple-element.25) | data formatting | bytes 1048576 | tf_op jit(solution)/shard_map/slice | solution.py:309
  35.4 0.2 copy.70
  35.6 0.0 copy-start.2
  35.6 1.3 copy.63
  36.9 0.2 copy.68
  37.1 0.0 collective-permute-done
  37.2 0.1 collective-permute-start.1
  37.3 2.2 %constant_dynamic-update-slice_fusion.1 = bf16[2,512,1024]{2,0,1:T(2,128)(2,1)} fusion(bf16[2,512,1024]{2,0,1:T(2,128)(2,1)} %get-tuple-element.28, bf16[2,128,1024]{2,0,1:T(2,128)(2,1)} %collective-permute-done), kind=kLoop, calls=%fused_computation.49 | loop fusion | bytes 1048576
  39.5 0.0 collective-permute-done.1
  39.5 1.1 constant_dynamic-update-slice_fusion
  40.6 3.2 %gather_fusion.1 = bf16[128,2,1024]{2,1,0:T(2,128)(2,1)S(1)} fusion(bf16[2,512,1024]{2,0,1:T(2,128)(2,1)} %constant_dynamic-update-slice_fusion, s32[1024]{0:T(1024)S(1)} %pad_clamp_fusion), kind=kCustom, calls=%fused_computation.1.clone | custom fusion | bytes 1049088 | tf_op jit(solution)/shard_map/jit(_take)/gather | solution.py:305
  43.9 3.2 %gather_fusion = bf16[128,2,1024]{2,1,0:T(2,128)(2,1)S(1)} fusion(bf16[2,512,1024]{2,0,1:T(2,128)(2,1)} %constant_dynamic-update-slice_fusion, s32[1024]{0:T(1024)S(1)} %pad_clamp_fusion.1), kind=kCustom, calls=%fused_computation.clone | custom fusion | bytes 1049088 | tf_op jit(solution)/shard_map/jit(_take)/gather | solution.py:304
  47.1 0.3 bitcast_convert_fusion
  47.4 0.0 slice-start
  47.4 0.4 fusion.10
  47.8 0.2 fusion.11
  47.9 0.0 slice-start.1
  47.9 0.0 slice-start.2
  47.9 6.5 %fusion.19 = f32[128,2048]{1,0:T(8,128)S(1)} fusion(bf16[2048,2048]{1,0:T(8,128)(2,1)} %constant.139.clone, f32[128,1024]{1,0:T(8,128)S(1)} %fusion.11, f32[128,1024]{1,0:T(8,128)S(1)} %get-tuple-element.18), kind=kOutput, calls=%fused_computation.47 | convolution fusion | flops 1074528256 | bytes 10485760 | tf_op jit(solution)/shard_map/dot_general | solution.py:317
  54.5 0.0 slice-done
  54.5 0.0 slice-done.1
  54.5 0.0 slice-start.3
  54.5 2.9 %convolution_add_fusion.1 = f32[128,2048]{1,0:T(8,128)S(1)} fusion(f32[128,2048]{1,0:T(8,128)S(1)} %fusion.19, bf16[2048,2048]{1,0:T(8,128)(2,1)S(1)} %bitcast.40, f32[128,1024]{1,0:T(8,128)S(1)} %fusion.11, f32[128,1024]{1,0:T(8,128)S(1)} %get-tuple-element.18), kind=kOutput, calls=%fused_computation.3 | convolution fusion | flops 1075052544 | bytes 11534336 | tf_op jit(solution)/shard_map/dot_general | solution.py:317
  57.4 0.0 slice-done.2
  57.4 0.0 copy-start.4
  57.4 3.1 %fusion.1 = bf16[2048,128]{0,1:T(8,128)(2,1)S(1)} fusion(f32[128,2048]{1,0:T(8,128)S(1)} %convolution_add_fusion.1, bf16[2048,2048]{1,0:T(8,128)(2,1)S(1)} %bitcast.42, f32[128,1024]{1,0:T(8,128)S(1)} %fusion.11, f32[128,1024]{1,0:T(8,128)S(1)} %get-tuple-element.18), kind=kOutput, calls=%fused_computation.5 | convolution fusion | flops 1075052544 | bytes 11010048 | tf_op jit(solution)/shard_map/dot_general | solution.py:317
  60.6 0.8 copy.74
  61.4 0.0 all-gather.5.cloned.1.call-update
  61.4 0.0 all-gather.7.cloned.1.call-start
  61.5 10.5 %all-gather.1 = s32[8,1,128]{2,1,0:T(1,128)S(1)} all-gather(s32[1,1,128]{2,1,0:T(1,128)S(1)} %bitcast.50), channel_id=1, replica_groups=mesh['row'=4,'stn'=2,'chan'=4] {'row','stn'}, dimensions={0}, use_global_device_ids=true | all-gather | bytes 4608 | tf_op jit(solution)/shard_map/all_gather | solution.py:300
  72.0 1.7 dynamic-slice_bitcast_fusion.refs_1_
  73.7 2.5 %fusion.16 = (bf16[1024,128]{1,0:T(8,128)(2,1)S(1)}, bf16[1024,128]{1,0:T(8,128)(2,1)S(1)}, bf16[1024,128]{1,0:T(8,128)(2,1)S(1)}) fusion(s32[1024]{0:T(1024)S(1)} %get-tuple-element.34), kind=kLoop, calls=%fused_computation.43 | loop fusion | flops 2359296 | bytes 790528 | tf_op jit(solution)/shard_map/convert.5
  76.2 1.1 maximum_maximum_fusion.refs_4_
  77.3 3.2 %fusion.17 = (f32[128,1024]{1,0:T(8,128)}, f32[128,1024]{1,0:T(8,128)}) fusion(s32[1024]{0:T(1024)S(1)} %get-tuple-element.35, s32[128]{0:T(128)S(1)} %and_select_fusion), kind=kLoop, calls=%fused_computation.44 | loop fusion | flops 1835008 | bytes 1053184 | tf_op jit(solution)/shard_map/sin | solution.py:348
  80.5 0.9 copy.73
  81.4 0.0 all-gather.7.cloned.1.call-update
  81.4 6.3 %all-gather.5.cloned.1.call-done.refs_0_ = bf16[8,12,64,128]{3,2,1,0:T(8,128)(2,1)} async-done(((bf16[1,12,64,128]{3,2,1,0:T(8,128)(2,1)}), bf16[8,12,64,128]{3,2,1,0:T(8,128)(2,1)}) %all-gather.5.cloned.1.call-update) | async-done | bytes 1572880 | tf_op jit(solution)/shard_map/all_gather | solution.py:326
  87.8 25.8 %early_rows.1.refs_6_ = f32[2,12,512,128]{3,2,1,0:T(8,128)} custom-call(bf16[8,12,64,128]{3,2,1,0:T(8,128)(2,1)} %all-gather.5.cloned.1.call-done.refs_0_, bf16[1024,128]{1,0:T(8,128)(2,1)} %dynamic-slice_bitcast_fusion.refs_1_, f32[128,1024]{1,0:T(8,128)} %get-tuple-element.14.refs_2_, f32[128,1024]{1,0:T(8,128)} %get-tuple-element.15.refs_3_, ...), custom_call_target="tpu_custom_call" | custom-call | flops 25769803776 | bytes 16777216 | tf_op jit(solution)/shard_map/early_rows/pallas_call | solution.py:236
  113.6 6.3 %all-gather.7.cloned.1.call-done = bf16[160,64,128]{2,1,0:T(8,128)(2,1)} async-done(((bf16[20,64,128]{2,1,0:T(8,128)(2,1)}), bf16[160,64,128]{2,1,0:T(8,128)(2,1)}) %all-gather.7.cloned.1.call-update) | async-done | bytes 2621456 | tf_op jit(solution)/shard_map/all_gather | solution.py:350
  119.9 56.4 %late_rows_to_sky.1 = f32[2,512,4096]{2,1,0:T(8,128)} custom-call(bf16[8,20,64,128]{3,2,1,0:T(8,128)(2,1)} %bitcast.43, bf16[1024,128]{1,0:T(8,128)(2,1)} %dynamic-slice_bitcast_fusion.refs_1_, f32[128,1024]{1,0:T(8,128)} %get-tuple-element.14.refs_2_, f32[128,1024]{1,0:T(8,128)} %get-tuple-element.15.refs_3_, ...), custom_call_target="tpu_custom_call" | custom-call | tf_op jit(solution)/shard_map/late_rows_to_sky/pallas_call | solution.py:257
  (18 shorter events, 0.1 us)
Async XLA Ops:
  6.5 81.2 %all-gather.5.cloned.1.call-start = ((), (), s32[]{:S(2)}) async-start(), calls=%async_computation | async-start | bytes 1769472 | tf_op jit(solution)/shard_map/all_gather | solution.py:326
  6.5 8.1 %copy-start.3 = (s32[128]{0:T(128)S(1)}, s32[128]{0:T(128)}, u32[]{:S(2)}) copy-start(s32[128]{0:T(128)} %param.17) | copy-start | bytes 1540
  6.5 8.2 %copy-start = (f32[2,128,640]{2,1,0:T(8,128)S(1)}, f32[2,128,640]{2,1,0:T(8,128)}, u32[]{:S(2)}) copy-start(f32[2,128,640]{2,1,0:T(8,128)} %vis_ref.1) | copy-start | bytes 1966084
  6.5 8.2 %copy-start.1 = (f32[2,128,640]{2,1,0:T(8,128)S(1)}, f32[2,128,640]{2,1,0:T(8,128)}, u32[]{:S(2)}) copy-start(f32[2,128,640]{2,1,0:T(8,128)} %off_ref.1) | copy-start | bytes 1966084
  11.7 25.5 %collective-permute-start = (bf16[2,128,1024]{2,0,1:T(2,128)(2,1)}, bf16[2,128,1024]{2,0,1:T(2,128)(2,1)}, u32[]{:S(2)}, u32[]{:S(2)}) collective-permute-start(bf16[2,128,1024]{2,0,1:T(2,128)(2,1)} %constant_dynamic-slice_fusion), channel_id=1, source_target_pairs={{0,4},{4,0},{1,5},{5,1},{2,6},{6,2},{3,7},{7,3},{8,12},{12,8},{9,1... | collective-permute-start | bytes 1572872 | tf_op jit(solution)/shard_map/ppermute | solution.py:285
  35.6 1.5 copy-start.2
  37.2 2.3 %collective-permute-start.1 = (bf16[2,128,1024]{2,0,1:T(2,128)(2,1)}, bf16[2,128,1024]{2,0,1:T(2,128)(2,1)S(1)}, u32[]{:S(2)}, u32[]{:S(2)}) collective-permute-start(bf16[2,128,1024]{2,0,1:T(2,128)(2,1)} %collective-permute-done), channel_id=1, source_target_pairs={{0,8},{8,0},{16,24},{24,16},{1,9},{9,1},{17,25},{25,17},{2,10},{10... | collective-permute-start | bytes 1572872 | tf_op jit(solution)/shard_map/ppermute | solution.py:286
  47.4 7.1 %slice-start = ((s8[8388608]{0:T(1024)(128)(4,1)}), s8[4194304]{0:T(1024)(128)(4,1)S(1)}, s32[]{:S(2)}) async-start(s8[8388608]{0:T(1024)(128)(4,1)} %bitcast.39), calls=%async_computation.2 | async-start | bytes 8388608
  47.9 6.6 %slice-start.1 = ((s8[8388608]{0:T(1024)(128)(4,1)}), s8[4194304]{0:T(1024)(128)(4,1)S(1)}, s32[]{:S(2)}) async-start(s8[8388608]{0:T(1024)(128)(4,1)} %bitcast.39), calls=%async_computation.3 | async-start | bytes 8388608
  47.9 9.5 %slice-start.2 = ((s8[8388608]{0:T(1024)(128)(4,1)}), s8[4194304]{0:T(1024)(128)(4,1)S(1)}, s32[]{:S(2)}) async-start(s8[8388608]{0:T(1024)(128)(4,1)} %bitcast.41), calls=%async_computation.4 | async-start | bytes 8388608
  54.5 2.9 %slice-start.3 = ((s8[8388608]{0:T(1024)(128)(4,1)}), s8[4194304]{0:T(1024)(128)(4,1)S(1)}, s32[]{:S(2)}) async-start(s8[8388608]{0:T(1024)(128)(4,1)} %bitcast.41), calls=%async_computation.5 | async-start | bytes 8388608
  57.4 4.1 %copy-start.4 = (s32[128]{0:T(128)S(1)}, s32[128]{0:T(128)}, u32[]{:S(2)}) copy-start(s32[128]{0:T(128)} %param.16) | copy-start | bytes 1540
  61.4 58.5 %all-gather.7.cloned.1.call-start = ((), (), s32[]{:S(2)}) async-start(), calls=%async_computation.1 | async-start | bytes 2949120 | tf_op jit(solution)/shard_map/all_gather | solution.py:350
Sparse Core Ops, SparseCore 0:
  61.5 26.1 all-gather.4
  89.7 30.2 all-gather.6
